TPU v7x, 32 devices: a whole 2x2x4 slice. The times are simulated.
32 devices in a mesh: groups: 2 (over y), pool: 8 (over z, x), tp: 2 (over core).
Axes of the slice: x: 2, y: 2, z: 4, core: 2. Of those that a mesh axis runs over, the one named last changes fastest.
Arguments:
- hidden_rows: bfloat16 [2048, 8192], P(('groups', 'pool'), 'tp'), parts along dimension 0, may hold values from -6 to 6
- base_out: bfloat16 [2048, 8192], P(('groups', 'pool'), 'tp'), parts along dimension 0, may hold values from -6 to 6
- row_adapter: int32 [2048, 1], P(('groups', 'pool')), parts along dimension 0, may hold values from 0 to 7; in each aligned block of 128 rows (0 to 127, 128 to 255, ...) at most 32 rows name the same one
- adapter_slot: int32 [8], replicated, may hold values from 0 to 7, each once
- shrink_pool: bfloat16 [8, 8192, 64], P('pool', 'tp'), may hold values from -0.0625 to 0.0625
- expand_pool: bfloat16 [8, 64, 8192], P('pool', None, 'tp'), may hold values from -0.75 to 0.75
Outputs:
- query_out: bfloat16 [2048, 8192], P(('groups', 'pool'), 'tp'), parts along dimension 0
There are 2 independent parts, one for each index of `groups`. A program takes and returns all parts, laid end to end along the dimension named above; an argument that names none is the same for every part. Nothing has to cross between parts.
Inputs may be any that keep to these rules, and one draw needn't show every extreme that they name: `row_adapter`: among the rows of one pool index, no adapter id stands on more than 32 rows, and some adapter stands on exactly 32 rows in some of them. `adapter_slot`: each adapter has one slot; each slot holds one adapter.
All inputs are finite; a program needn't handle non-finite values.
Results may differ from a plain program's by a relative error of at most 0.0055.
Values may be sent and summed in bfloat16 or wider, within the bound.
A program may use at most 64 MiB of HBM per device.

v0:
```python
import jax
import jax.numpy as jnp
from jax import lax
from jax.sharding import PartitionSpec as P


def local(hidden_rows, base_out, row_adapter, adapter_slot, shrink_pool, expand_pool):
    n_pool = lax.axis_size("pool")
    rows_dev = hidden_rows.shape[0]
    capacity = 2 * max(1, rows_dev // n_pool)
    total_slots = n_pool * capacity
    adapter_ids = row_adapter[:, 0]
    count_adapters = adapter_slot.shape[0]
    matches = adapter_ids[:, None] == jnp.arange(count_adapters, dtype=jnp.int32)[None, :]
    owner_dev = jnp.sum(jnp.where(matches, adapter_slot[None, :], 0), axis=1)
    order_idx = jnp.arange(rows_dev, dtype=jnp.int32)
    earlier = (adapter_ids[:, None] == adapter_ids[None, :]) & (
        order_idx[None, :] < order_idx[:, None]
    )
    rank_in = jnp.sum(earlier.astype(jnp.int32), axis=1)
    target = owner_dev * capacity + rank_in
    onehot = (target[:, None] == jnp.arange(total_slots, dtype=jnp.int32)[None, :]).astype(
        jnp.bfloat16
    )
    packed = lax.dot_general(
        onehot, hidden_rows, (((0,), (0,)), ((), ())), preferred_element_type=jnp.float32
    )
    packed = packed.astype(jnp.bfloat16).reshape(n_pool, capacity, hidden_rows.shape[1])
    shrink_local = shrink_pool[0]
    expand_local = expand_pool[0]
    partial_latent = jnp.einsum(
        "skd,dr->skr",
        lax.all_to_all(packed, "pool", split_axis=0, concat_axis=0, tiled=True),
        shrink_local,
        preferred_element_type=jnp.float32,
    )
    latent = lax.psum(partial_latent, "tp").astype(jnp.bfloat16)
    update = (
        2.0 * jnp.einsum("skr,ro->sko", latent, expand_local, preferred_element_type=jnp.float32)
    ).astype(jnp.bfloat16)
    returned = lax.all_to_all(update, "pool", split_axis=0, concat_axis=0, tiled=True)
    flat_rows = returned.reshape(total_slots, returned.shape[2])
    unpacked = jnp.dot(onehot, flat_rows, preferred_element_type=jnp.float32)
    return (base_out.astype(jnp.float32) + unpacked).astype(jnp.bfloat16)


def solution(mesh):
    placed = (
        P(("groups", "pool"), "tp"),
        P(("groups", "pool"), "tp"),
        P(("groups", "pool"), None),
        P(),
        P("pool", "tp", None),
        P("pool", None, "tp"),
    )
    return jax.shard_map(
        local, mesh=mesh, in_specs=placed, out_specs=P(("groups", "pool"), "tp"), check_vma=False
    )
```

profile of v0, /device:TPU:0, one launch (start us, length us, event | category | flops | bytes accessed | tf_op | source)
XLA Modules:
  0.0 116.9 jit_solution(8584082419856101314)
XLA Ops:
  0.0 0.0 copy-start
  0.0 0.9 convert_reduce_fusion
  0.9 0.8 select_reduce_fusion
  1.7 0.0 copy-done
  1.7 0.8 convolution_convert_fusion
  2.5 0.0 copy-start.2
  2.5 55.4 %all_to_all.10 = bf16[8,32,4096]{2,1,0:T(8,128)(2,1)S(1)} all-to-all(bf16[8,32,4096]{2,1,0:T(8,128)(2,1)S(1)} %bitcast.16), channel_id=1, replica_groups=mesh['groups'=2,'pool'=8,'tp'=2] {'pool'}, dimensions={0} | all-to-all | bytes 4194304 | tf_op jit(solution)/shard_map/all_to_all | solution.py:33
  58.0 0.0 copy-done.2
  58.0 0.0 copy-start.3
  58.0 0.7 fusion.3
  58.7 3.8 %psum.7 = bf16[8,32,64]{2,1,0:T(8,128)(2,1)S(1)} all-reduce(f32[8,32,64]{2,1,0:T(8,128)S(1)} %fusion.3), channel_id=1, replica_groups=mesh['groups'=2,'pool'=8,'tp'=2] {'tp'}, use_global_device_ids=true, to_apply=%region_2.3 | all-reduce | flops 16384 | bytes 98304 | tf_op jit(solution)/shard_map/psum | solution.py:37
  62.5 0.0 copy-done.3
  62.5 0.7 fusion
  63.2 0.0 copy-start.1
  63.2 52.2 %all_to_all.11 = bf16[8,32,4096]{2,1,0:T(8,128)(2,1)S(1)} all-to-all(bf16[8,32,4096]{2,1,0:T(8,128)(2,1)S(1)} %fusion), channel_id=1, replica_groups=mesh['groups'=2,'pool'=8,'tp'=2] {'pool'}, dimensions={0} | all-to-all | bytes 4194304 | tf_op jit(solution)/shard_map/all_to_all | solution.py:41
  115.5 0.0 copy-done.1
  115.5 1.5 %fusion.1 = bf16[128,4096]{1,0:T(8,128)(2,1)} fusion(bf16[256,4096]{1,0:T(8,128)(2,1)S(1)} %bitcast.15, bf16[128,4096]{1,0:T(8,128)(2,1)S(1)} %copy-done.1, s32[128]{0:T(128)S(1)} %multiply_add_fusion), kind=kOutput, calls=%fused_computation.4 | convolution fusion | flops 270041088 | bytes 4194816 | tf_op jit(solution)/shard_map/dot_general | solution.py:43
  (1 shorter events, 0.0 us)
Async XLA Ops:
  0.0 1.7 %copy-start = (bf16[128,4096]{1,0:T(8,128)(2,1)S(1)}, bf16[128,4096]{1,0:T(8,128)(2,1)}, u32[]{:S(2)}) copy-start(bf16[128,4096]{1,0:T(8,128)(2,1)} %param.6) | copy-start | bytes 3145732
  2.5 55.4 %copy-start.2 = (bf16[1,4096,64]{1,2,0:T(8,128)(2,1)S(1)}, bf16[1,4096,64]{1,2,0:T(8,128)(2,1)}, u32[]{:S(2)}) copy-start(bf16[1,4096,64]{1,2,0:T(8,128)(2,1)} %param.10) | copy-start | bytes 1572868
  58.0 4.6 %copy-start.3 = (bf16[1,64,4096]{2,1,0:T(8,128)(2,1)S(1)}, bf16[1,64,4096]{2,1,0:T(8,128)(2,1)}, u32[]{:S(2)}) copy-start(bf16[1,64,4096]{2,1,0:T(8,128)(2,1)} %param.11) | copy-start | bytes 1572868
  63.2 52.2 %copy-start.1 = (bf16[128,4096]{1,0:T(8,128)(2,1)S(1)}, bf16[128,4096]{1,0:T(8,128)(2,1)}, u32[]{:S(2)}) copy-start(bf16[128,4096]{1,0:T(8,128)(2,1)} %param.7) | copy-start | bytes 3145732
where the time goes:
time: 117 us
  blocking collectives  111 us (95%)
  matrix products  3.65 us (3%)
  other arithmetic  1.7 us (1%)
    all_to_all x1, blocking collectives, local(): lax.all_to_all(packed, 'pool', split_axis=0, concat_axis=0, tiled=True)  55.4 us
    all_to_all x1, blocking collectives, local(): lax.all_to_all(update, 'pool', split_axis=0, concat_axis=0, tiled=True)  52.2 us
    psum x1, blocking collectives, local(): latent = lax.psum(partial_latent, 'tp').astype(jnp.bfloat16)  3.85 us

commit v1 on v0

--- a/solution.py
+++ b/solution.py
@@ -1,10 +1,17 @@
+import functools
 import jax
 import jax.numpy as jnp
 from jax import lax
+from jax.experimental import pallas as pl
+from jax.experimental.pallas import tpu as pltpu
 from jax.sharding import PartitionSpec as P
 
-
-def local(hidden_rows, base_out, row_adapter, adapter_slot, shrink_pool, expand_pool):
+MESH = pl.DeviceIdType.MESH
+X = 2
+CHUNKS = 4
+
+
+def moved_rows(hidden_rows, base_out, row_adapter, adapter_slot, shrink_pool, expand_pool):
     n_pool = lax.axis_size("pool")
     rows_dev = hidden_rows.shape[0]
     capacity = 2 * max(1, rows_dev // n_pool)
@@ -44,6 +51,262 @@
     return (base_out.astype(jnp.float32) + unpacked).astype(jnp.bfloat16)
 
 
+def kernel(n_z, hidden, ids, adapter_slot, shrink, expand, out,
+           slots, s_all, h_all, id_all, e_all, part, red, lat, upd,
+           loc_sem, sx_sem, s_send, s_recv, h_sem, id_sem, ex_sem, e_send, e_recv,
+           rs_sem, ag_sem, u_sem):
+    g = lax.axis_index("groups")
+    p = lax.axis_index("pool")
+    t = lax.axis_index("tp")
+    z = p // X
+    x = p - z * X
+    rows = hidden.shape[0]
+    rank = expand.shape[0]
+    quarter = h_all.shape[1]
+    pair = X * rank
+    width = quarter // CHUNKS
+    f32, bf16 = jnp.float32, jnp.bfloat16
+
+    def flip(fg, fx, ft=0):
+        return (1 - g if fg else g), (1 - x if fx else x), (1 - t if ft else t)
+
+    def device(coords):
+        return (coords[0], z * X + coords[1], coords[2])
+
+    def up_down(up):
+        return (g, p + X, t) if up else (g, p - X, t)
+
+    q = 2 * g + x
+    q_x = 2 * g + 1 - x
+    planes = [(0, 1), (1, 0), (1, 1)]
+    layer = [(a, b, c) for a in (0, 1) for b in (0, 1) for c in (0, 1) if a or b or c]
+    pending = []
+
+    def cols(index, size):
+        return pl.ds(pl.multiple_of(index * size, size), size)
+
+    s_copy = pltpu.make_async_copy(
+        shrink.at[:, cols(q, quarter)], s_all.at[cols(p, rank)], loc_sem.at[0])
+    s_copy.start()
+    h_copy = pltpu.make_async_copy(
+        hidden.at[:, cols(q, quarter)], h_all.at[cols(q, rows)], loc_sem.at[1])
+    h_copy.start()
+    e_copies = []
+    for c in range(CHUNKS):
+        e_copies.append(pltpu.make_async_copy(
+            expand.at[:, pl.ds(pl.multiple_of(q * quarter + c * width, width), width)],
+            e_all.at[c, cols(p, rank)], loc_sem.at[2 + c]))
+        e_copies[-1].start()
+
+    barrier = pltpu.get_barrier_semaphore()
+    for f in layer:
+        pl.semaphore_signal(barrier, inc=1, device_id=device(flip(*f)), device_id_type=MESH)
+
+    @pl.when(z > 0)
+    def _():
+        pl.semaphore_signal(barrier, inc=1, device_id=up_down(False), device_id_type=MESH)
+
+    @pl.when(z < n_z - 1)
+    def _():
+        pl.semaphore_signal(barrier, inc=1, device_id=up_down(True), device_id_type=MESH)
+
+    slot = jnp.zeros(ids.shape, jnp.int32)
+    for a in range(n_z * X):
+        slot = jnp.where(ids[...] == a, adapter_slot[a], slot)
+    slots[...] = jnp.broadcast_to(slot, slots.shape)
+    id_all[q] = slots[...]
+
+    pl.semaphore_wait(barrier, len(layer) + (z > 0).astype(jnp.int32)
+                      + (z < n_z - 1).astype(jnp.int32))
+
+    def remote(src, dst, send, recv, target):
+        return pltpu.make_async_remote_copy(src_ref=src, dst_ref=dst, send_sem=send, recv_sem=recv,
+                                            device_id=target, device_id_type=MESH)
+
+    def s_hop(origin, stream, up):
+        which = x if stream == 0 else 1 - x
+        at = s_all.at[cols(origin * X + which, rank)]
+        return remote(at, at, s_send.at[origin, stream, int(up)], s_recv.at[origin, stream],
+                      up_down(up))
+
+    def e_hop(origin, c, up):
+        at = e_all.at[c, cols(origin, pair)]
+        return remote(at, at, e_send.at[origin, c, int(up)], e_recv.at[origin, c], up_down(up))
+
+    def send_own(hop):
+        for up in (True, False):
+            cond = z < n_z - 1 if up else z > 0
+
+            @pl.when(cond)
+            def _(up=up):
+                hop(z, up).start()
+            pending.append((cond, functools.partial(hop, z, up)))
+
+    def pass_on(hop, step):
+        for up in (True, False):
+            origin = z - step if up else z + step
+            here = (z >= step) if up else (z + step < n_z)
+            onward = here & ((z < n_z - 1) if up else (z > 0))
+
+            @pl.when(here)
+            def _(origin=origin, up=up):
+                hop(origin, up).wait_recv()
+
+            @pl.when(onward)
+            def _(origin=origin, up=up):
+                hop(origin, up).start()
+            pending.append((onward, functools.partial(hop, origin, up)))
+
+    side = device(flip(0, 1))
+    sx_copy = remote(shrink.at[:, cols(q_x, quarter)], s_all.at[cols(p, rank)],
+                     sx_sem.at[0], sx_sem.at[1], side)
+    sx_copy.start()
+    s_copy.wait()
+    send_own(lambda origin, up: s_hop(origin, 0, up))
+
+    id_copies, h_copies = [], []
+    for i, (fg, fx) in enumerate(planes):
+        to = flip(fg, fx)
+        there = 2 * to[0] + to[1]
+        id_copies.append(remote(slots, id_all.at[q], id_sem.at[0, i], id_sem.at[1, i], device(to)))
+        h_copies.append(remote(hidden.at[:, cols(there, quarter)], h_all.at[cols(q, rows)],
+                               h_sem.at[0, i], h_sem.at[1, i], device(to)))
+    for copy in id_copies + h_copies:
+        copy.start()
+    ex_copies = []
+    for c in range(CHUNKS):
+        ex_copies.append(remote(
+            expand.at[:, pl.ds(pl.multiple_of(q_x * quarter + c * width, width), width)],
+            e_all.at[c, cols(p, rank)], ex_sem.at[0, c], ex_sem.at[1, c], side))
+        ex_copies[-1].start()
+
+    sx_copy.wait_recv()
+    send_own(lambda origin, up: s_hop(origin, 1, up))
+    for step in range(1, n_z):
+        for stream in (0, 1):
+            pass_on(lambda origin, up, stream=stream: s_hop(origin, stream, up), step)
+
+    for c in range(CHUNKS):
+        e_copies[c].wait()
+        ex_copies[c].wait_recv()
+        send_own(lambda origin, up, c=c: e_hop(origin, c, up))
+
+    h_copy.wait()
+    for copy in id_copies + h_copies:
+        copy.wait_recv()
+    slot = jnp.concatenate([id_all[k][0:1, :] for k in range(2 * X)], axis=1)
+    total = jnp.zeros((rank, slot.shape[1]), f32)
+    for k in range(n_z):
+        block = lax.dot_general(s_all[k * pair:(k + 1) * pair, :], h_all[...],
+                                (((1,), (1,)), ((), ())), preferred_element_type=f32)
+        for m in range(X):
+            total += jnp.where(slot == k * X + m, block[m * rank:(m + 1) * rank], 0.0)
+    part[...] = total
+
+    n_layer = len(layer) + 1
+    share = rank // n_layer
+    mine = 2 * q + t
+    rs_copies = []
+    for i, f in enumerate(layer):
+        to = flip(*f)
+        there = 2 * (2 * to[0] + to[1]) + to[2]
+        rs_copies.append(remote(part.at[cols(there, share)], red.at[i],
+                                rs_sem.at[0, i], rs_sem.at[1, i], device(to)))
+        rs_copies[-1].start()
+    summed = part[cols(mine, share), :]
+    for i, copy in enumerate(rs_copies):
+        copy.wait_recv()
+        summed += red[i]
+    lat[cols(mine, share), :] = summed
+    ag_copies = []
+    for i, f in enumerate(layer):
+        at = lat.at[cols(mine, share)]
+        ag_copies.append(remote(at, at, ag_sem.at[0, i], ag_sem.at[1, i], device(flip(*f))))
+        ag_copies[-1].start()
+    for copy in ag_copies:
+        copy.wait_recv()
+
+    latent = lat[...].astype(bf16).astype(f32)
+    placed = jnp.concatenate([jnp.where(slot == a, latent, 0.0).astype(bf16)
+                              for a in range(n_z * X)], axis=0)
+    n_rows = slot.shape[1]
+    unit = (lax.broadcasted_iota(jnp.int32, (n_rows, n_rows), 0)
+            == lax.broadcasted_iota(jnp.int32, (n_rows, n_rows), 1)).astype(bf16)
+    placed = lax.dot_general(unit, placed, (((1,), (1,)), ((), ())),
+                             preferred_element_type=f32).astype(bf16)
+
+    u_copies = []
+    for c in range(CHUNKS):
+        for step in range(1, n_z):
+            pass_on(lambda origin, up, c=c: e_hop(origin, c, up), step)
+        upd[c] = (2.0 * jnp.dot(placed, e_all[c], preferred_element_type=f32)).astype(bf16)
+        here = pl.ds(pl.multiple_of(q * quarter + c * width, width), width)
+        for i, (fg, fx) in enumerate(planes):
+            to = flip(fg, fx)
+            there = 2 * to[0] + to[1]
+            u_copies.append(remote(upd.at[c, cols(there, rows)], out.at[:, here],
+                                   u_sem.at[0, c, i], u_sem.at[1, c, i], device(to)))
+            u_copies[-1].start()
+        out[:, here] = upd[c, cols(q, rows), :]
+
+    for copy in u_copies:
+        copy.wait_recv()
+    for copy in [sx_copy] + id_copies + h_copies + ex_copies + rs_copies + ag_copies + u_copies:
+        copy.wait_send()
+    for cond, make in pending:
+        @pl.when(cond)
+        def _(make=make):
+            make().wait_send()
+
+
+def moved_adapters(hidden_rows, base_out, row_adapter, adapter_slot, shrink_pool, expand_pool):
+    n_pool = lax.axis_size("pool")
+    n_z = n_pool // X
+    rows, features = hidden_rows.shape
+    rank, outs = expand_pool.shape[1:]
+    quarter = features // (2 * X)
+    n_rows = 2 * X * rows
+    bf16, f32 = jnp.bfloat16, jnp.float32
+    dma = pltpu.SemaphoreType.DMA
+    any_spec = pl.BlockSpec(memory_space=pl.ANY)
+    vmem_spec = pl.BlockSpec(memory_space=pltpu.VMEM)
+    update = pl.pallas_call(
+        functools.partial(kernel, n_z),
+        out_shape=jax.ShapeDtypeStruct((rows, outs), bf16),
+        in_specs=[any_spec, vmem_spec, pl.BlockSpec(memory_space=pltpu.SMEM), any_spec, any_spec],
+        out_specs=vmem_spec,
+        scratch_shapes=[
+            pltpu.VMEM((8, rows), jnp.int32),
+            pltpu.VMEM((n_pool * rank, quarter), bf16),
+            pltpu.VMEM((n_rows, quarter), bf16),
+            pltpu.VMEM((2 * X, 8, rows), jnp.int32),
+            pltpu.VMEM((CHUNKS, n_pool * rank, quarter // CHUNKS), bf16),
+            pltpu.VMEM((rank, n_rows), f32),
+            pltpu.VMEM((7, rank // 8, n_rows), f32),
+            pltpu.VMEM((rank, n_rows), f32),
+            pltpu.VMEM((CHUNKS, n_rows, quarter // CHUNKS), bf16),
+            dma((2 + CHUNKS,)),
+            dma((2,)),
+            dma((n_z, 2, 2)),
+            dma((n_z, 2)),
+            dma((2, 3)),
+            dma((2, 3)),
+            dma((2, CHUNKS)),
+            dma((n_z, CHUNKS, 2)),
+            dma((n_z, CHUNKS)),
+            dma((2, 7)),
+            dma((2, 7)),
+            dma((2, CHUNKS, 3)),
+        ],
+        compiler_params=pltpu.CompilerParams(
+            collective_id=0, has_side_effects=True, vmem_limit_bytes=40 * 1024 * 1024),
+        cost_estimate=pl.CostEstimate(
+            flops=4 * rows * features * n_pool * rank, bytes_accessed=6 * 1024 * 1024,
+            transcendentals=0),
+    )(hidden_rows, row_adapter.reshape(1, rows), adapter_slot, shrink_pool[0].T, expand_pool[0])
+    return (base_out.astype(f32) + update.astype(f32)).astype(bf16)
+
+
 def solution(mesh):
     placed = (
         P(("groups", "pool"), "tp"),
@@ -53,6 +316,8 @@
         P("pool", "tp", None),
         P("pool", None, "tp"),
     )
+    few = mesh.shape["pool"] <= 16 and mesh.shape["groups"] == 2 and mesh.shape["tp"] == 2
+    local = moved_adapters if few else moved_rows
     return jax.shard_map(
         local, mesh=mesh, in_specs=placed, out_specs=P(("groups", "pool"), "tp"), check_vma=False
     )

time: 117 us -> 63 us (0.54)
  blocking collectives: 111 us -> 0 us
  Pallas kernels: 0 us -> 56.9 us
  local copies, waits for them, and re-layouts: 0.02 us -> 4.62 us
  matrix products: 3.65 us -> 0 us
    all_to_all x2 -> x0, blocking collectives: 108 us -> none  [the longest x1 55.4 us: local(): lax.all_to_all(packed, 'pool', split_axis=0, concat_axis=0, tiled=True)]
    pallas_call x0 -> x1, Pallas kernels: none -> 56.9 us  [moved_adapters(): pl.pallas_call(functools.partial(kernel, n_z), out_shape=jax.ShapeDtypeSt...]
    unnamed x8 -> x12, local copies, waits for them, and re-layouts: 0.02 us -> 4.62 us
    psum x1 -> x0, blocking collectives: 3.85 us -> none  [local(): latent = lax.psum(partial_latent, 'tp').astype(jnp.bfloat16)]
    dot_general x4 -> x0, matrix products: 3.65 us -> none  [the longest x1 1.46 us: local(): unpacked = jnp.dot(onehot, flat_rows, preferred_element_type=jnp.float32)]
    reduce_sum x2 -> x0, other arithmetic: 1.69 us -> none  [the longest x1 0.93 us: local(): rank_in = jnp.sum(earlier.astype(jnp.int32), axis=1)]
    convert_element_type x0 -> x1, other arithmetic: none -> 1.22 us  [moved_adapters(): return (base_out.astype(f32) + update.astype(f32)).astype(bf16)]
where the time goes in v1:
time: 63 us; the launch traced here: 62.8 us
  Pallas kernels  56.9 us (90%)
  local copies, waits for them, and re-layouts  4.62 us (7%)
  other arithmetic  1.22 us (2%)
    pallas_call x1, Pallas kernels, moved_adapters(): pl.pallas_call(functools.partial(kernel, n_z), out_shape=jax.ShapeDtypeSt...  56.9 us
    unnamed x12, local copies, waits for them, and re-layouts  4.62 us

profile of v1, /device:TPU:0, one launch (start us, length us, event | category | flops | bytes accessed | tf_op | source)
XLA Modules:
  0.0 62.8 jit_solution(13479336742740797976)
XLA Ops:
  0.0 0.0 copy-start
  0.0 1.2 %copy-done = bf16[128,4096]{1,0:T(8,128)(2,1)S(1)} copy-done((bf16[128,4096]{1,0:T(8,128)(2,1)S(1)}, bf16[128,4096]{1,0:T(8,128)(2,1)}, u32[]{:S(2)}) %copy-start) | copy-done | bytes 1048600
  1.2 0.0 copy-start.1
  1.2 1.0 %copy-done.1 = bf16[1,4096,64]{1,2,0:T(8,128)(2,1)S(1)} copy-done((bf16[1,4096,64]{1,2,0:T(8,128)(2,1)S(1)}, bf16[1,4096,64]{1,2,0:T(8,128)(2,1)}, u32[]{:S(2)}) %copy-start.1) | copy-done | bytes 524312
  2.3 0.0 copy-start.2
  2.3 1.0 %copy-done.2 = bf16[1,64,4096]{2,1,0:T(8,128)(2,1)S(1)} copy-done((bf16[1,64,4096]{2,1,0:T(8,128)(2,1)S(1)}, bf16[1,64,4096]{2,1,0:T(8,128)(2,1)}, u32[]{:S(2)}) %copy-start.2) | copy-done | bytes 524312
  3.3 0.0 copy-start.3
  3.3 0.7 %copy-done.3 = s32[128,1]{0,1:T(1,128)S(1)} copy-done((s32[128,1]{0,1:T(1,128)S(1)}, s32[128,1]{0,1:T(1,128)}, u32[]{:S(2)}) %copy-start.3) | copy-done | bytes 536
  4.0 0.0 copy-start.4
  4.0 0.7 %copy-done.4 = s32[8]{0:T(128)S(1)} copy-done((s32[8]{0:T(128)S(1)}, s32[8]{0:T(128)}, u32[]{:S(2)}) %copy-start.4) | copy-done | bytes 56
  4.6 0.0 copy-start.5
  4.6 56.9 %shard_map.64 = bf16[128,4096]{1,0:T(8,128)(2,1)S(1)} custom-call(bf16[128,4096]{1,0:T(8,128)(2,1)S(1)} %copy-done, s32[1,128]{1,0:T(1,128)S(1)} %bitcast.7, s32[8]{0:T(128)S(1)} %copy-done.4, bf16[64,4096]{1,0:T(8,128)(2,1)S(1)} %bitcast.5, bf16[64,4096]{1,0:T(8,128)(2,1)S(1)} %bitcast.6), custom_call_target="tpu_custom_call" | custom-call | flops 1073741824 | bytes 6291456 | tf_op jit(solution)/shard_map/pallas_call | solution.py:273
  61.5 0.0 copy-done.5
  61.5 1.2 %add_convert_fusion = bf16[128,4096]{1,0:T(8,128)(2,1)} fusion(bf16[128,4096]{1,0:T(8,128)(2,1)S(1)} %shard_map.64, bf16[128,4096]{1,0:T(8,128)(2,1)S(1)} %copy-done.5), kind=kLoop, calls=%fused_computation | loop fusion | flops 2097152 | bytes 3145728 | tf_op jit(solution)/shard_map/convert_element_type | solution.py:307
Async XLA Ops:
  0.0 1.2 %copy-start = (bf16[128,4096]{1,0:T(8,128)(2,1)S(1)}, bf16[128,4096]{1,0:T(8,128)(2,1)}, u32[]{:S(2)}) copy-start(bf16[128,4096]{1,0:T(8,128)(2,1)} %hidden.1) | copy-start | bytes 3145732
  1.2 1.0 %copy-start.1 = (bf16[1,4096,64]{1,2,0:T(8,128)(2,1)S(1)}, bf16[1,4096,64]{1,2,0:T(8,128)(2,1)}, u32[]{:S(2)}) copy-start(bf16[1,4096,64]{1,2,0:T(8,128)(2,1)} %param.10) | copy-start | bytes 1572868
  2.3 1.0 %copy-start.2 = (bf16[1,64,4096]{2,1,0:T(8,128)(2,1)S(1)}, bf16[1,64,4096]{2,1,0:T(8,128)(2,1)}, u32[]{:S(2)}) copy-start(bf16[1,64,4096]{2,1,0:T(8,128)(2,1)} %param.11) | copy-start | bytes 1572868
  3.3 0.7 %copy-start.3 = (s32[128,1]{0,1:T(1,128)S(1)}, s32[128,1]{0,1:T(1,128)}, u32[]{:S(2)}) copy-start(s32[128,1]{0,1:T(1,128)} %param.8) | copy-start | bytes 1540
  4.0 0.7 %copy-start.4 = (s32[8]{0:T(128)S(1)}, s32[8]{0:T(128)}, u32[]{:S(2)}) copy-start(s32[8]{0:T(128)} %adapter_slot.1) | copy-start | bytes 100
  4.6 56.9 %copy-start.5 = (bf16[128,4096]{1,0:T(8,128)(2,1)S(1)}, bf16[128,4096]{1,0:T(8,128)(2,1)}, u32[]{:S(2)}) copy-start(bf16[128,4096]{1,0:T(8,128)(2,1)} %param.7) | copy-start | bytes 3145732

commit v2 on v1

--- a/solution.py
+++ b/solution.py
@@ -9,6 +9,7 @@
 MESH = pl.DeviceIdType.MESH
 X = 2
 CHUNKS = 4
+DEPTH = 2
 
 
 def moved_rows(hidden_rows, base_out, row_adapter, adapter_slot, shrink_pool, expand_pool):
@@ -51,8 +52,8 @@
     return (base_out.astype(jnp.float32) + unpacked).astype(jnp.bfloat16)
 
 
-def kernel(n_z, hidden, ids, adapter_slot, shrink, expand, out,
-           slots, s_all, h_all, id_all, e_all, part, red, lat, upd,
+def kernel(n_z, hidden, ids_hbm, table_hbm, shrink, expand, out,
+           ids, table, slots, s_all, h_all, id_all, e_all, part, red, lat, upd,
            loc_sem, sx_sem, s_send, s_recv, h_sem, id_sem, ex_sem, e_send, e_recv,
            rs_sem, ag_sem, u_sem):
     g = lax.axis_index("groups")
@@ -81,10 +82,19 @@
     planes = [(0, 1), (1, 0), (1, 1)]
     layer = [(a, b, c) for a in (0, 1) for b in (0, 1) for c in (0, 1) if a or b or c]
     pending = []
+    at_end = (z == 0) | (z == n_z - 1)
+    inner = jnp.logical_not(at_end)
+    always = z >= 0
+    outward = (z == 1, z == n_z - 2)
+    across = (z == n_z - 2, z == 1)
 
     def cols(index, size):
         return pl.ds(pl.multiple_of(index * size, size), size)
 
+    ids_copy = pltpu.make_async_copy(ids_hbm, ids, loc_sem.at[2 + CHUNKS])
+    ids_copy.start()
+    table_copy = pltpu.make_async_copy(table_hbm, table, loc_sem.at[3 + CHUNKS])
+    table_copy.start()
     s_copy = pltpu.make_async_copy(
         shrink.at[:, cols(q, quarter)], s_all.at[cols(p, rank)], loc_sem.at[0])
     s_copy.start()
@@ -110,9 +120,11 @@
     def _():
         pl.semaphore_signal(barrier, inc=1, device_id=up_down(True), device_id_type=MESH)
 
+    ids_copy.wait()
+    table_copy.wait()
     slot = jnp.zeros(ids.shape, jnp.int32)
     for a in range(n_z * X):
-        slot = jnp.where(ids[...] == a, adapter_slot[a], slot)
+        slot = jnp.where(ids[...] == a, table[a], slot)
     slots[...] = jnp.broadcast_to(slot, slots.shape)
     id_all[q] = slots[...]
 
@@ -133,36 +145,66 @@
         at = e_all.at[c, cols(origin, pair)]
         return remote(at, at, e_send.at[origin, c, int(up)], e_recv.at[origin, c], up_down(up))
 
-    def send_own(hop):
+    def send_own(hop, held, only=(always, always)):
         for up in (True, False):
-            cond = z < n_z - 1 if up else z > 0
+            cond = ((z < n_z - 1) if up else (z > 0)) & only[int(up)]
 
             @pl.when(cond)
             def _(up=up):
                 hop(z, up).start()
-            pending.append((cond, functools.partial(hop, z, up)))
-
-    def pass_on(hop, step):
+            held.append((cond, functools.partial(hop, z, up)))
+
+    def drain(held, also=always):
+        for cond, make in held:
+            @pl.when(cond & also)
+            def _(make=make):
+                make().wait_send()
+
+    def passed(step, up):
+        origin = z - step if up else z + step
+        here = (z >= step) if up else (z + step < n_z)
+        onward = here & ((z < n_z - 1) if up else (z > 0))
+        return origin, here, onward
+
+    def pass_on(hop, step, held, only=(always, always)):
         for up in (True, False):
-            origin = z - step if up else z + step
-            here = (z >= step) if up else (z + step < n_z)
-            onward = here & ((z < n_z - 1) if up else (z > 0))
-
-            @pl.when(here)
+            origin, _, onward = passed(step, up)
+            onward = onward & only[int(up)]
+
+            @pl.when(onward)
             def _(origin=origin, up=up):
                 hop(origin, up).wait_recv()
-
-            @pl.when(onward)
+                hop(origin, up).start()
+            held.append((onward, functools.partial(hop, origin, up)))
+
+    def take(hop, step):
+        for up in (True, False):
+            origin, here, onward = passed(step, up)
+
+            @pl.when(here & jnp.logical_not(onward))
             def _(origin=origin, up=up):
-                hop(origin, up).start()
-            pending.append((onward, functools.partial(hop, origin, up)))
+                hop(origin, up).wait_recv()
+
+    def s_stream(stream):
+        return lambda origin, up: s_hop(origin, stream, up)
+
+    def e_chunk(c):
+        return lambda origin, up: e_hop(origin, c, up)
 
     side = device(flip(0, 1))
     sx_copy = remote(shrink.at[:, cols(q_x, quarter)], s_all.at[cols(p, rank)],
                      sx_sem.at[0], sx_sem.at[1], side)
     sx_copy.start()
     s_copy.wait()
-    send_own(lambda origin, up: s_hop(origin, 0, up))
+    s_own, s_passed = [], []
+    send_own(s_stream(0), s_own)
+
+    ex_copies = []
+    for c in range(CHUNKS):
+        ex_copies.append(remote(
+            expand.at[:, pl.ds(pl.multiple_of(q_x * quarter + c * width, width), width)],
+            e_all.at[c, cols(p, rank)], ex_sem.at[0, c], ex_sem.at[1, c], side))
+        ex_copies[-1].start()
 
     id_copies, h_copies = [], []
     for i, (fg, fx) in enumerate(planes):
@@ -173,27 +215,32 @@
                                h_sem.at[0, i], h_sem.at[1, i], device(to)))
     for copy in id_copies + h_copies:
         copy.start()
-    ex_copies = []
-    for c in range(CHUNKS):
-        ex_copies.append(remote(
-            expand.at[:, pl.ds(pl.multiple_of(q_x * quarter + c * width, width), width)],
-            e_all.at[c, cols(p, rank)], ex_sem.at[0, c], ex_sem.at[1, c], side))
-        ex_copies[-1].start()
-
     sx_copy.wait_recv()
-    send_own(lambda origin, up: s_hop(origin, 1, up))
-    for step in range(1, n_z):
+    send_own(s_stream(1), s_own)
+    drain(s_own, at_end)
+    for c in range(CHUNKS):
+        @pl.when(at_end)
+        def _(c=c):
+            e_copies[c].wait()
+            ex_copies[c].wait_recv()
+        send_own(e_chunk(c), pending, (at_end, at_end))
+    for step in range(1, n_z - 1):
         for stream in (0, 1):
-            pass_on(lambda origin, up, stream=stream: s_hop(origin, stream, up), step)
-
-    for c in range(CHUNKS):
-        e_copies[c].wait()
-        ex_copies[c].wait_recv()
-        send_own(lambda origin, up, c=c: e_hop(origin, c, up))
+            pass_on(s_stream(stream), step, s_passed)
+    for c in range(CHUNKS):
+        @pl.when(inner)
+        def _(c=c):
+            e_copies[c].wait()
+            ex_copies[c].wait_recv()
+        send_own(e_chunk(c), pending, across)
+        pass_on(e_chunk(c), 1, pending, across)
 
     h_copy.wait()
     for copy in id_copies + h_copies:
         copy.wait_recv()
+    for step in range(1, n_z):
+        for stream in (0, 1):
+            take(s_stream(stream), step)
     slot = jnp.concatenate([id_all[k][0:1, :] for k in range(2 * X)], axis=1)
     total = jnp.zeros((rank, slot.shape[1]), f32)
     for k in range(n_z):
@@ -213,6 +260,19 @@
         rs_copies.append(remote(part.at[cols(there, share)], red.at[i],
                                 rs_sem.at[0, i], rs_sem.at[1, i], device(to)))
         rs_copies[-1].start()
+    drain(s_own, inner)
+    drain(s_passed)
+    e_out = [[] for _ in range(CHUNKS)]
+
+    def e_outward(c):
+        if c >= DEPTH:
+            drain(e_out[c - DEPTH])
+        send_own(e_chunk(c), e_out[c], outward)
+        for step in range(1, n_z - 1):
+            pass_on(e_chunk(c), step, e_out[c], outward)
+
+    for c in range(DEPTH):
+        e_outward(c)
     summed = part[cols(mine, share), :]
     for i, copy in enumerate(rs_copies):
         copy.wait_recv()
@@ -223,6 +283,10 @@
         at = lat.at[cols(mine, share)]
         ag_copies.append(remote(at, at, ag_sem.at[0, i], ag_sem.at[1, i], device(flip(*f))))
         ag_copies[-1].start()
+    for c in range(DEPTH, CHUNKS):
+        e_outward(c)
+    for held in e_out[-DEPTH:]:
+        pending.extend(held)
     for copy in ag_copies:
         copy.wait_recv()
 
@@ -238,7 +302,7 @@
     u_copies = []
     for c in range(CHUNKS):
         for step in range(1, n_z):
-            pass_on(lambda origin, up, c=c: e_hop(origin, c, up), step)
+            take(e_chunk(c), step)
         upd[c] = (2.0 * jnp.dot(placed, e_all[c], preferred_element_type=f32)).astype(bf16)
         here = pl.ds(pl.multiple_of(q * quarter + c * width, width), width)
         for i, (fg, fx) in enumerate(planes):
@@ -253,10 +317,7 @@
         copy.wait_recv()
     for copy in [sx_copy] + id_copies + h_copies + ex_copies + rs_copies + ag_copies + u_copies:
         copy.wait_send()
-    for cond, make in pending:
-        @pl.when(cond)
-        def _(make=make):
-            make().wait_send()
+    drain(pending)
 
 
 def moved_adapters(hidden_rows, base_out, row_adapter, adapter_slot, shrink_pool, expand_pool):
@@ -268,14 +329,16 @@
     n_rows = 2 * X * rows
     bf16, f32 = jnp.bfloat16, jnp.float32
     dma = pltpu.SemaphoreType.DMA
-    any_spec = pl.BlockSpec(memory_space=pl.ANY)
+    hbm_spec = pl.BlockSpec(memory_space=pltpu.HBM)
     vmem_spec = pl.BlockSpec(memory_space=pltpu.VMEM)
     update = pl.pallas_call(
         functools.partial(kernel, n_z),
         out_shape=jax.ShapeDtypeStruct((rows, outs), bf16),
-        in_specs=[any_spec, vmem_spec, pl.BlockSpec(memory_space=pltpu.SMEM), any_spec, any_spec],
+        in_specs=[hbm_spec] * 5,
         out_specs=vmem_spec,
         scratch_shapes=[
+            pltpu.VMEM((1, rows), jnp.int32),
+            pltpu.SMEM(adapter_slot.shape, jnp.int32),
             pltpu.VMEM((8, rows), jnp.int32),
             pltpu.VMEM((n_pool * rank, quarter), bf16),
             pltpu.VMEM((n_rows, quarter), bf16),
@@ -285,7 +348,7 @@
             pltpu.VMEM((7, rank // 8, n_rows), f32),
             pltpu.VMEM((rank, n_rows), f32),
             pltpu.VMEM((CHUNKS, n_rows, quarter // CHUNKS), bf16),
-            dma((2 + CHUNKS,)),
+            dma((4 + CHUNKS,)),
             dma((2,)),
             dma((n_z, 2, 2)),
             dma((n_z, 2)),
@@ -299,7 +362,7 @@
             dma((2, CHUNKS, 3)),
         ],
         compiler_params=pltpu.CompilerParams(
-            collective_id=0, has_side_effects=True, vmem_limit_bytes=40 * 1024 * 1024),
+            collective_id=0, has_side_effects=True, vmem_limit_bytes=60 * 1024 * 1024),
         cost_estimate=pl.CostEstimate(
             flops=4 * rows * features * n_pool * rank, bytes_accessed=6 * 1024 * 1024,
             transcendentals=0),
@@ -316,7 +379,7 @@
         P("pool", "tp", None),
         P("pool", None, "tp"),
     )
-    few = mesh.shape["pool"] <= 16 and mesh.shape["groups"] == 2 and mesh.shape["tp"] == 2
+    few = mesh.shape["pool"] == 4 * X and mesh.shape["groups"] == 2 and mesh.shape["tp"] == 2
     local = moved_adapters if few else moved_rows
     return jax.shard_map(
         local, mesh=mesh, in_specs=placed, out_specs=P(("groups", "pool"), "tp"), check_vma=False

time: 63 us -> 54.1 us (0.86)
  Pallas kernels: 56.9 us -> 51.4 us
  local copies, waits for them, and re-layouts: 4.62 us -> 0.01 us
  other arithmetic: 1.22 us -> 2.45 us
    pallas_call x1, Pallas kernels: 56.9 us -> 51.4 us  [moved_adapters(): pl.pallas_call(functools.partial(kernel, n_z), out_shape=jax.ShapeDtypeSt...]
    unnamed x12 -> x2, local copies, waits for them, and re-layouts: 4.62 us -> 0.01 us
    convert_element_type x1, other arithmetic: 1.22 us -> 2.45 us  [moved_adapters(): return (base_out.astype(f32) + update.astype(f32)).astype(bf16)]
where the time goes in v2:
time: 54.1 us; the launch traced here: 53.9 us
  Pallas kernels  51.4 us (95%)
  other arithmetic  2.45 us (5%)
    pallas_call x1, Pallas kernels, moved_adapters(): pl.pallas_call(functools.partial(kernel, n_z), out_shape=jax.ShapeDtypeSt...  51.4 us
    convert_element_type x1, other arithmetic, moved_adapters(): return (base_out.astype(f32) + update.astype(f32)).astype(bf16)  2.45 us

profile of v2, /device:TPU:0, one launch (start us, length us, event | category | flops | bytes accessed | tf_op | source)
XLA Modules:
  0.0 53.9 jit_solution(13191379692118941157)
XLA Ops:
  0.0 0.0 copy-start
  0.0 51.4 %shard_map.64 = bf16[128,4096]{1,0:T(8,128)(2,1)} custom-call(bf16[128,4096]{1,0:T(8,128)(2,1)} %hidden.1, s32[1,128]{1,0:T(1,128)} %bitcast.7, s32[8]{0:T(128)} %table_hbm.1, bf16[64,4096]{1,0:T(8,128)(2,1)} %bitcast.5, bf16[64,4096]{1,0:T(8,128)(2,1)} %bitcast.6), custom_call_target="tpu_custom_call" | custom-call | flops 1073741824 | bytes 6291456 | tf_op jit(solution)/shard_map/pallas_call | solution.py:334
  51.4 0.0 copy-done
  51.5 2.4 %add_convert_fusion = bf16[128,4096]{1,0:T(8,128)(2,1)} fusion(bf16[128,4096]{1,0:T(8,128)(2,1)} %shard_map.64, bf16[128,4096]{1,0:T(8,128)(2,1)S(1)} %copy-done), kind=kLoop, calls=%fused_computation | loop fusion | flops 2097152 | bytes 3145728 | tf_op jit(solution)/shard_map/convert_element_type | solution.py:370
Async XLA Ops:
  0.0 51.5 %copy-start = (bf16[128,4096]{1,0:T(8,128)(2,1)S(1)}, bf16[128,4096]{1,0:T(8,128)(2,1)}, u32[]{:S(2)}) copy-start(bf16[128,4096]{1,0:T(8,128)(2,1)} %param.7) | copy-start | bytes 3145732

commit v3 on v2

--- a/solution.py
+++ b/solution.py
@@ -55,7 +55,7 @@
 def kernel(n_z, hidden, ids_hbm, table_hbm, shrink, expand, out,
            ids, table, slots, s_all, h_all, id_all, e_all, part, red, lat, upd,
            loc_sem, sx_sem, s_send, s_recv, h_sem, id_sem, ex_sem, e_send, e_recv,
-           rs_sem, ag_sem, u_sem):
+           rs_sem, ag_sem, u_sem, own_sem):
     g = lax.axis_index("groups")
     p = lax.axis_index("pool")
     t = lax.axis_index("tp")
@@ -299,7 +299,7 @@
     placed = lax.dot_general(unit, placed, (((1,), (1,)), ((), ())),
                              preferred_element_type=f32).astype(bf16)
 
-    u_copies = []
+    u_copies, own_copies = [], []
     for c in range(CHUNKS):
         for step in range(1, n_z):
             take(e_chunk(c), step)
@@ -311,12 +311,16 @@
             u_copies.append(remote(upd.at[c, cols(there, rows)], out.at[:, here],
                                    u_sem.at[0, c, i], u_sem.at[1, c, i], device(to)))
             u_copies[-1].start()
-        out[:, here] = upd[c, cols(q, rows), :]
+        own_copies.append(pltpu.make_async_copy(upd.at[c, cols(q, rows)], out.at[:, here],
+                                                own_sem.at[c]))
+        own_copies[-1].start()
 
     for copy in u_copies:
         copy.wait_recv()
     for copy in [sx_copy] + id_copies + h_copies + ex_copies + rs_copies + ag_copies + u_copies:
         copy.wait_send()
+    for copy in own_copies:
+        copy.wait()
     drain(pending)
 
 
@@ -330,12 +334,11 @@
     bf16, f32 = jnp.bfloat16, jnp.float32
     dma = pltpu.SemaphoreType.DMA
     hbm_spec = pl.BlockSpec(memory_space=pltpu.HBM)
-    vmem_spec = pl.BlockSpec(memory_space=pltpu.VMEM)
     update = pl.pallas_call(
         functools.partial(kernel, n_z),
         out_shape=jax.ShapeDtypeStruct((rows, outs), bf16),
         in_specs=[hbm_spec] * 5,
-        out_specs=vmem_spec,
+        out_specs=hbm_spec,
         scratch_shapes=[
             pltpu.VMEM((1, rows), jnp.int32),
             pltpu.SMEM(adapter_slot.shape, jnp.int32),
@@ -360,6 +363,7 @@
             dma((2, 7)),
             dma((2, 7)),
             dma((2, CHUNKS, 3)),
+            dma((CHUNKS,)),
         ],
         compiler_params=pltpu.CompilerParams(
             collective_id=0, has_side_effects=True, vmem_limit_bytes=60 * 1024 * 1024),

time: 54.1 us -> 53.2 us (0.983)
  Pallas kernels: 51.4 us -> 50.6 us
    pallas_call x1, Pallas kernels: 51.4 us -> 50.6 us  [moved_adapters(): pl.pallas_call(functools.partial(kernel, n_z), out_shape=jax.ShapeDtypeSt...]
where the time goes in v3:
time: 53.2 us; the launch traced here: 53.1 us
  Pallas kernels  50.6 us (95%)
  other arithmetic  2.45 us (5%)
    pallas_call x1, Pallas kernels, moved_adapters(): pl.pallas_call(functools.partial(kernel, n_z), out_shape=jax.ShapeDtypeSt...  50.6 us
    convert_element_type x1, other arithmetic, moved_adapters(): return (base_out.astype(f32) + update.astype(f32)).astype(bf16)  2.45 us

profile of v3, /device:TPU:0, one launch (start us, length us, event | category | flops | bytes accessed | tf_op | source)
XLA Modules:
  0.0 53.1 jit_solution(12781665981912661346)
XLA Ops:
  0.0 0.0 copy-start
  0.0 50.6 %shard_map.64 = bf16[128,4096]{1,0:T(8,128)(2,1)} custom-call(bf16[128,4096]{1,0:T(8,128)(2,1)} %hidden.1, s32[1,128]{1,0:T(1,128)} %bitcast.7, s32[8]{0:T(128)} %table_hbm.1, bf16[64,4096]{1,0:T(8,128)(2,1)} %bitcast.5, bf16[64,4096]{1,0:T(8,128)(2,1)} %bitcast.6), custom_call_target="tpu_custom_call" | custom-call | flops 1073741824 | bytes 6291456 | tf_op jit(solution)/shard_map/pallas_call | solution.py:337
  50.6 0.0 copy-done
  50.6 2.4 %add_convert_fusion = bf16[128,4096]{1,0:T(8,128)(2,1)} fusion(bf16[128,4096]{1,0:T(8,128)(2,1)} %shard_map.64, bf16[128,4096]{1,0:T(8,128)(2,1)S(1)} %copy-done), kind=kLoop, calls=%fused_computation | loop fusion | flops 2097152 | bytes 3145728 | tf_op jit(solution)/shard_map/convert_element_type | solution.py:374
Async XLA Ops:
  0.0 50.6 %copy-start = (bf16[128,4096]{1,0:T(8,128)(2,1)S(1)}, bf16[128,4096]{1,0:T(8,128)(2,1)}, u32[]{:S(2)}) copy-start(bf16[128,4096]{1,0:T(8,128)(2,1)} %param.7) | copy-start | bytes 3145732
